TPU v7x, 32 devices: a whole 2x2x4 slice. The times are simulated.
32 devices in a mesh: grow: 8 (over z, x), wide: 4 (over y, core).
Axes of the slice: x: 2, y: 2, z: 4, core: 2. Of those that a mesh axis runs over, the one named last changes fastest.
Arguments:
- fields: float32 [3, 128, 128, 128], P(None, 'grow', 'wide'), may hold values from -1 to 1
- melt_planes: float32 [3, 16, 128, 128], P(None, None, 'wide'), may hold values from -1 to 1
- slide_planes: int32 [8], replicated, may hold values from 0 to 8, as said below
Outputs:
- evolved: float32 [3, 128, 128, 128], P(None, 'grow', 'wide')
Inputs may be any that keep to these rules, and one draw needn't show every extreme that they name: `slide_planes`: entries at even positions k are 0; at least one entry equals 8, and at most one other entry is nonzero.
All inputs are finite; a program needn't handle non-finite values.
Results may differ from a plain program's by a relative error of at most 0.0001.
Values sent between devices are 32-bit elements; how exact they have to be, the bound alone decides.
No kernel may reach another device: no remote copies, remote signals or barrier semaphores. Data moves between devices by JAX's collectives and lax.ppermute only.
A program may use at most 64 MiB of HBM per device.

v0:
```python
import jax
import jax.numpy as jnp
from jax import lax
from jax.sharding import PartitionSpec as P

SUBSTEPS = 8


coef_phase = 0.15
coef_react = 0.3
coef_couple = 0.4
coef_solute = 1.5
coef_diff = 0.1
coef_heat = 0.16


def passed_along(value, axis, steps):
    count = lax.axis_size(axis)
    leading, last = (max(0, -steps), min(count, count - steps))
    return lax.ppermute(value, axis, [(source, source + steps) for source in range(leading, last)])


def with_halo(block, sides, width):
    for axis, dim in sides:
        count = lax.axis_size(axis)
        forward = [(i, i + 1) for i in range(count - 1)]
        backward = [(target, source) for source, target in forward]
        low = lax.ppermute(
            lax.slice_in_dim(block, block.shape[dim] - width, None, axis=dim), axis, forward
        )
        high = lax.ppermute(lax.slice_in_dim(block, 0, width, axis=dim), axis, backward)
        block = jnp.concatenate([low, block, high], axis=dim)
    return block


def advance(padded):
    centre = padded[:, 1:-1, 1:-1]
    laplace = (
        padded[:, 2:, 1:-1]
        + padded[:, :-2, 1:-1]
        + padded[:, 1:-1, 2:]
        + padded[:, 1:-1, :-2]
        + jnp.roll(centre, 1, 3)
        + jnp.roll(centre, -1, 3)
        - 6.0 * centre
    )
    phase_now, solute, thermal = (centre[0], centre[1], centre[2])
    squared = 1.0 - phase_now * phase_now
    driving = (
        phase_now
        + coef_phase * laplace[0]
        + coef_react * (phase_now - phase_now * phase_now * phase_now)
        - coef_couple * squared * squared * (thermal + coef_solute * solute)
    )
    grown = jnp.tanh(driving)
    change = 0.5 * (grown - phase_now)
    solute_next = solute + coef_diff * laplace[1] + change
    thermal_next = thermal + coef_heat * laplace[2] + change
    return jnp.stack([grown, solute_next, thermal_next])


def inside_mask(rows, cols):
    grow_total = rows * lax.axis_size("grow")
    wide_total = cols * lax.axis_size("wide")
    grow_index = lax.axis_index("grow") * rows - 1 + jnp.arange(rows + 2, dtype=jnp.int32)
    wide_index = lax.axis_index("wide") * cols - 1 + jnp.arange(cols + 2, dtype=jnp.int32)
    grow_inside = (grow_index >= 0) & (grow_index < grow_total)
    wide_inside = (wide_index >= 0) & (wide_index < wide_total)
    inside = (grow_inside[:, None] & wide_inside[None, :]).astype(jnp.float32)
    return inside[None, :, :, None]


def slide_block(state, melt_planes, shift, cursor):
    rows = state.shape[1]
    at_end = lax.axis_index("grow") == lax.axis_size("grow") - 1
    piece = state[:, : rows // 2]
    melt_piece = lax.dynamic_slice_in_dim(melt_planes, cursor, rows // 2, 1)
    received = passed_along(piece, "grow", -1)
    incoming = jnp.where(at_end, melt_piece, received)
    combined = jnp.concatenate([state, incoming], 1)
    return lax.dynamic_slice_in_dim(combined, shift, rows, 1)


def body(fields, melt_planes, slide_planes):
    rows = fields.shape[1]
    cols = fields.shape[2]
    state = fields
    inside = inside_mask(rows, cols)
    for pair_index in range(SUBSTEPS // 2):
        padded = with_halo(state, (("grow", 1), ("wide", 2)), 2)
        middle = advance(padded) * inside
        state = advance(middle)
        substep = 2 * pair_index + 1
        shift = slide_planes[substep]
        cursor = jnp.sum(slide_planes[:substep])
        state = slide_block(state, melt_planes, shift, cursor)
    return state


def solution(mesh):
    return jax.shard_map(
        body,
        mesh=mesh,
        in_specs=(P(None, "grow", "wide", None), P(None, None, "wide", None), P()),
        out_specs=P(None, "grow", "wide", None),
        check_vma=False,
    )
```

profile of v0, /device:TPU:1, one launch (start us, length us, event | category | flops | bytes accessed | tf_op | source)
XLA Modules:
  0.0 138.4 jit_solution(11452653651405784974)
XLA Ops:
  0.0 1.0 fusion.152
  1.0 4.0 %collective-permute-start = (f32[3,2,32,128]{3,2,1,0:T(8,128)S(1)}, f32[3,2,32,128]{3,2,1,0:T(8,128)S(1)}, u32[]{:S(2)}, u32[]{:S(2)}) collective-permute-start(f32[3,2,32,128]{3,2,1,0:T(8,128)S(1)} %get-tuple-element.68), channel_id=1, source_target_pairs={{0,4},{4,8},{8,12},{12,16},{16,20},{20,24},{24,28},{1,5},{5,9},{9,... | collective-permute-start | bytes 294920 | tf_op jit(solution)/shard_map/ppermute | solution.py:28
  4.9 1.3 collective-permute-start.1
  6.5 1.2 constant_dynamic-update-slice_fusion.1
  7.7 2.5 %collective-permute-done.1 = f32[3,2,32,128]{3,2,1,0:T(8,128)S(1)} collective-permute-done((f32[3,2,32,128]{3,2,1,0:T(8,128)S(1)}, f32[3,2,32,128]{3,2,1,0:T(8,128)S(1)}, u32[]{:S(2)}, u32[]{:S(2)}) %collective-permute-start.1) | collective-permute-done | bytes 98336 | tf_op jit(solution)/shard_map/ppermute | solution.py:31
  10.3 4.0 %collective-permute-start.3 = (f32[3,20,2,128]{3,2,1,0:T(2,128)S(1)}, f32[3,20,2,128]{3,2,1,0:T(2,128)S(1)}, u32[]{:S(2)}, u32[]{:S(2)}) collective-permute-start(f32[3,20,2,128]{3,2,1,0:T(2,128)S(1)} %get-tuple-element.60), channel_id=1, source_target_pairs={{1,0},{2,1},{3,2},{5,4},{6,5},{7,6},{9,8},{10,9},{11,10},{13,12},{... | collective-permute-start | bytes 184328 | tf_op jit(solution)/shard_map/ppermute | solution.py:31
  14.4 3.0 %collective-permute-start.2 = (f32[3,20,2,128]{3,2,1,0:T(2,128)S(1)}, f32[3,20,2,128]{3,2,1,0:T(2,128)S(1)}, u32[]{:S(2)}, u32[]{:S(2)}) collective-permute-start(f32[3,20,2,128]{3,2,1,0:T(2,128)S(1)} %get-tuple-element.59), channel_id=1, source_target_pairs={{0,1},{1,2},{2,3},{4,5},{5,6},{6,7},{8,9},{9,10},{10,11},{12,13},{... | collective-permute-start | bytes 184328 | tf_op jit(solution)/shard_map/ppermute | solution.py:28
  17.5 1.2 collective-permute-done.2
  18.9 0.4 fusion.138
  19.3 0.4 fusion.139
  19.6 0.9 fusion.15
  20.5 0.3 fusion.82
  21.5 0.3 fusion.147
  21.8 0.6 fusion.41
  22.8 1.4 %collective-permute-start.4 = (f32[3,8,32,128]{3,2,1,0:T(8,128)S(1)}, f32[3,8,32,128]{3,2,1,0:T(8,128)S(1)}, u32[]{:S(2)}, u32[]{:S(2)}) collective-permute-start(f32[3,8,32,128]{3,2,1,0:T(8,128)S(1)} %pad_maximum_fusion.30), channel_id=1, source_target_pairs={{4,0},{8,4},{12,8},{16,12},{20,16},{24,20},{28,24},{5,1},{9,5},{13... | collective-permute-start | bytes 1179656 | tf_op jit(solution)/shard_map/ppermute | solution.py:20
  24.3 0.7 fusion.153
  28.5 7.0 %collective-permute-done.4 = f32[3,8,32,128]{3,2,1,0:T(8,128)S(1)} collective-permute-done((f32[3,8,32,128]{3,2,1,0:T(8,128)S(1)}, f32[3,8,32,128]{3,2,1,0:T(8,128)S(1)}, u32[]{:S(2)}, u32[]{:S(2)}) %collective-permute-start.4) | collective-permute-done | bytes 393248 | tf_op jit(solution)/shard_map/ppermute | solution.py:20
  35.9 1.3 collective-permute-start.6
  37.2 5.2 %collective-permute-start.5 = (f32[3,2,32,128]{3,2,1,0:T(8,128)S(1)}, f32[3,2,32,128]{3,2,1,0:T(8,128)S(1)}, u32[]{:S(2)}, u32[]{:S(2)}) collective-permute-start(f32[3,2,32,128]{3,2,1,0:T(8,128)S(1)} %get-tuple-element.65), channel_id=1, source_target_pairs={{0,4},{4,8},{8,12},{12,16},{16,20},{20,24},{24,28},{1,5},{5,9},{9,... | collective-permute-start | bytes 294920 | tf_op jit(solution)/shard_map/ppermute | solution.py:28
  42.3 1.1 collective-permute-done.6
  43.5 2.5 %collective-permute-done.5 = f32[3,2,32,128]{3,2,1,0:T(8,128)S(1)} collective-permute-done((f32[3,2,32,128]{3,2,1,0:T(8,128)S(1)}, f32[3,2,32,128]{3,2,1,0:T(8,128)S(1)}, u32[]{:S(2)}, u32[]{:S(2)}) %collective-permute-start.5) | collective-permute-done | bytes 98336 | tf_op jit(solution)/shard_map/ppermute | solution.py:28
  46.0 2.4 %collective-permute-start.8 = (f32[3,20,2,128]{3,2,1,0:T(2,128)S(1)}, f32[3,20,2,128]{3,2,1,0:T(2,128)S(1)}, u32[]{:S(2)}, u32[]{:S(2)}) collective-permute-start(f32[3,20,2,128]{3,2,1,0:T(2,128)S(1)} %get-tuple-element.58), channel_id=1, source_target_pairs={{1,0},{2,1},{3,2},{5,4},{6,5},{7,6},{9,8},{10,9},{11,10},{13,12},{... | collective-permute-start | bytes 184328 | tf_op jit(solution)/shard_map/ppermute | solution.py:31
  48.4 3.2 %collective-permute-start.7 = (f32[3,20,2,128]{3,2,1,0:T(2,128)S(1)}, f32[3,20,2,128]{3,2,1,0:T(2,128)S(1)}, u32[]{:S(2)}, u32[]{:S(2)}) collective-permute-start(f32[3,20,2,128]{3,2,1,0:T(2,128)S(1)} %get-tuple-element.57), channel_id=1, source_target_pairs={{0,1},{1,2},{2,3},{4,5},{5,6},{6,7},{8,9},{9,10},{10,11},{12,13},{... | collective-permute-start | bytes 184328 | tf_op jit(solution)/shard_map/ppermute | solution.py:28
  51.6 1.3 collective-permute-done.7
  53.0 0.4 fusion.136
  53.4 0.4 fusion.137
  53.8 0.9 fusion.10
  54.7 0.3 fusion.77
  55.6 0.3 fusion.145
  56.0 0.6 fusion.38
  57.0 1.3 collective-permute-start.9
  59.6 0.6 slice_reduce_fusion.2
  62.8 6.7 %collective-permute-done.9 = f32[3,8,32,128]{3,2,1,0:T(8,128)S(1)} collective-permute-done((f32[3,8,32,128]{3,2,1,0:T(8,128)S(1)}, f32[3,8,32,128]{3,2,1,0:T(8,128)S(1)}, u32[]{:S(2)}, u32[]{:S(2)}) %collective-permute-start.9) | collective-permute-done | bytes 393248 | tf_op jit(solution)/shard_map/ppermute | solution.py:20
  69.8 1.3 collective-permute-start.11
  71.1 5.2 %collective-permute-start.10 = (f32[3,2,32,128]{3,2,1,0:T(8,128)S(1)}, f32[3,2,32,128]{3,2,1,0:T(8,128)S(1)}, u32[]{:S(2)}, u32[]{:S(2)}) collective-permute-start(f32[3,2,32,128]{3,2,1,0:T(8,128)S(1)} %get-tuple-element.63), channel_id=1, source_target_pairs={{0,4},{4,8},{8,12},{12,16},{16,20},{20,24},{24,28},{1,5},{5,9},{9,... | collective-permute-start | bytes 294920 | tf_op jit(solution)/shard_map/ppermute | solution.py:28
  76.2 1.2 collective-permute-done.11
  77.5 2.4 %collective-permute-done.10 = f32[3,2,32,128]{3,2,1,0:T(8,128)S(1)} collective-permute-done((f32[3,2,32,128]{3,2,1,0:T(8,128)S(1)}, f32[3,2,32,128]{3,2,1,0:T(8,128)S(1)}, u32[]{:S(2)}, u32[]{:S(2)}) %collective-permute-start.10) | collective-permute-done | bytes 98336 | tf_op jit(solution)/shard_map/ppermute | solution.py:28
  79.9 2.4 %collective-permute-start.13 = (f32[3,20,2,128]{3,2,1,0:T(2,128)S(1)}, f32[3,20,2,128]{3,2,1,0:T(2,128)S(1)}, u32[]{:S(2)}, u32[]{:S(2)}) collective-permute-start(f32[3,20,2,128]{3,2,1,0:T(2,128)S(1)} %get-tuple-element.56), channel_id=1, source_target_pairs={{1,0},{2,1},{3,2},{5,4},{6,5},{7,6},{9,8},{10,9},{11,10},{13,12},{... | collective-permute-start | bytes 184328 | tf_op jit(solution)/shard_map/ppermute | solution.py:31
  82.3 3.4 %collective-permute-start.12 = (f32[3,20,2,128]{3,2,1,0:T(2,128)S(1)}, f32[3,20,2,128]{3,2,1,0:T(2,128)S(1)}, u32[]{:S(2)}, u32[]{:S(2)}) collective-permute-start(f32[3,20,2,128]{3,2,1,0:T(2,128)S(1)} %get-tuple-element.55), channel_id=1, source_target_pairs={{0,1},{1,2},{2,3},{4,5},{5,6},{6,7},{8,9},{9,10},{10,11},{12,13},{... | collective-permute-start | bytes 184328 | tf_op jit(solution)/shard_map/ppermute | solution.py:28
  85.7 1.1 collective-permute-done.12
  87.0 0.4 fusion.134
  87.3 0.4 fusion.135
  87.7 0.9 fusion.5
  88.6 0.3 fusion.72
  89.9 0.6 fusion.35
  90.9 1.3 collective-permute-start.14
  93.3 0.6 slice_reduce_fusion.1
  96.4 7.0 %collective-permute-done.14 = f32[3,8,32,128]{3,2,1,0:T(8,128)S(1)} collective-permute-done((f32[3,8,32,128]{3,2,1,0:T(8,128)S(1)}, f32[3,8,32,128]{3,2,1,0:T(8,128)S(1)}, u32[]{:S(2)}, u32[]{:S(2)}) %collective-permute-start.14) | collective-permute-done | bytes 393248 | tf_op jit(solution)/shard_map/ppermute | solution.py:20
  103.7 1.3 collective-permute-start.16
  105.0 5.2 %collective-permute-start.15 = (f32[3,2,32,128]{3,2,1,0:T(8,128)S(1)}, f32[3,2,32,128]{3,2,1,0:T(8,128)S(1)}, u32[]{:S(2)}, u32[]{:S(2)}) collective-permute-start(f32[3,2,32,128]{3,2,1,0:T(8,128)S(1)} %get-tuple-element.61), channel_id=1, source_target_pairs={{0,4},{4,8},{8,12},{12,16},{16,20},{20,24},{24,28},{1,5},{5,9},{9,... | collective-permute-start | bytes 294920 | tf_op jit(solution)/shard_map/ppermute | solution.py:28
  110.1 1.2 collective-permute-done.16
  111.4 2.4 %collective-permute-done.15 = f32[3,2,32,128]{3,2,1,0:T(8,128)S(1)} collective-permute-done((f32[3,2,32,128]{3,2,1,0:T(8,128)S(1)}, f32[3,2,32,128]{3,2,1,0:T(8,128)S(1)}, u32[]{:S(2)}, u32[]{:S(2)}) %collective-permute-start.15) | collective-permute-done | bytes 98336 | tf_op jit(solution)/shard_map/ppermute | solution.py:28
  113.8 2.4 %collective-permute-start.18 = (f32[3,20,2,128]{3,2,1,0:T(2,128)S(1)}, f32[3,20,2,128]{3,2,1,0:T(2,128)S(1)}, u32[]{:S(2)}, u32[]{:S(2)}) collective-permute-start(f32[3,20,2,128]{3,2,1,0:T(2,128)S(1)} %get-tuple-element.54), channel_id=1, source_target_pairs={{1,0},{2,1},{3,2},{5,4},{6,5},{7,6},{9,8},{10,9},{11,10},{13,12},{... | collective-permute-start | bytes 184328 | tf_op jit(solution)/shard_map/ppermute | solution.py:31
  116.2 3.2 %collective-permute-start.17 = (f32[3,20,2,128]{3,2,1,0:T(2,128)S(1)}, f32[3,20,2,128]{3,2,1,0:T(2,128)S(1)}, u32[]{:S(2)}, u32[]{:S(2)}) collective-permute-start(f32[3,20,2,128]{3,2,1,0:T(2,128)S(1)} %get-tuple-element.53), channel_id=1, source_target_pairs={{0,1},{1,2},{2,3},{4,5},{5,6},{6,7},{8,9},{9,10},{10,11},{12,13},{... | collective-permute-start | bytes 184328 | tf_op jit(solution)/shard_map/ppermute | solution.py:28
  119.4 1.3 collective-permute-done.17
  120.9 0.4 fusion.132
  121.2 0.4 fusion.133
  121.6 0.9 fusion
  122.5 0.3 fusion.67
  123.8 0.6 fusion.32
  124.8 1.3 collective-permute-start.19
  127.4 0.6 slice_reduce_fusion
  130.6 6.7 %collective-permute-done.19 = f32[3,8,32,128]{3,2,1,0:T(8,128)S(1)} collective-permute-done((f32[3,8,32,128]{3,2,1,0:T(8,128)S(1)}, f32[3,8,32,128]{3,2,1,0:T(8,128)S(1)}, u32[]{:S(2)}, u32[]{:S(2)}) %collective-permute-start.19) | collective-permute-done | bytes 393248 | tf_op jit(solution)/shard_map/ppermute | solution.py:20
  137.3 1.1 fusion.22
  (58 shorter events, 6.7 us)
Async XLA Ops:
  1.0 5.6 %collective-permute-start = (f32[3,2,32,128]{3,2,1,0:T(8,128)S(1)}, f32[3,2,32,128]{3,2,1,0:T(8,128)S(1)}, u32[]{:S(2)}, u32[]{:S(2)}) collective-permute-start(f32[3,2,32,128]{3,2,1,0:T(8,128)S(1)} %get-tuple-element.68), channel_id=1, source_target_pairs={{0,4},{4,8},{8,12},{12,16},{16,20},{20,24},{24,28},{1,5},{5,9},{9,... | collective-permute-start | bytes 294920 | tf_op jit(solution)/shard_map/ppermute | solution.py:28
  4.9 5.4 %collective-permute-start.1 = (f32[3,2,32,128]{3,2,1,0:T(8,128)S(1)}, f32[3,2,32,128]{3,2,1,0:T(8,128)S(1)}, u32[]{:S(2)}, u32[]{:S(2)}) collective-permute-start(f32[3,2,32,128]{3,2,1,0:T(8,128)S(1)} %get-tuple-element.67), channel_id=1, source_target_pairs={{4,0},{8,4},{12,8},{16,12},{20,16},{24,20},{28,24},{5,1},{9,5},{13... | collective-permute-start | bytes 294920 | tf_op jit(solution)/shard_map/ppermute | solution.py:31
  10.3 7.2 %collective-permute-start.3 = (f32[3,20,2,128]{3,2,1,0:T(2,128)S(1)}, f32[3,20,2,128]{3,2,1,0:T(2,128)S(1)}, u32[]{:S(2)}, u32[]{:S(2)}) collective-permute-start(f32[3,20,2,128]{3,2,1,0:T(2,128)S(1)} %get-tuple-element.60), channel_id=1, source_target_pairs={{1,0},{2,1},{3,2},{5,4},{6,5},{7,6},{9,8},{10,9},{11,10},{13,12},{... | collective-permute-start | bytes 184328 | tf_op jit(solution)/shard_map/ppermute | solution.py:31
  14.4 4.3 %collective-permute-start.2 = (f32[3,20,2,128]{3,2,1,0:T(2,128)S(1)}, f32[3,20,2,128]{3,2,1,0:T(2,128)S(1)}, u32[]{:S(2)}, u32[]{:S(2)}) collective-permute-start(f32[3,20,2,128]{3,2,1,0:T(2,128)S(1)} %get-tuple-element.59), channel_id=1, source_target_pairs={{0,1},{1,2},{2,3},{4,5},{5,6},{6,7},{8,9},{9,10},{10,11},{12,13},{... | collective-permute-start | bytes 184328 | tf_op jit(solution)/shard_map/ppermute | solution.py:28
  22.7 1.6 %copy-start.1 = (s32[8]{0:T(128)S(1)}, s32[8]{0:T(128)}, u32[]{:S(2)}) copy-start(s32[8]{0:T(128)} %param.5) | copy-start | bytes 100
  22.7 12.9 %copy-start = (f32[3,16,32,128]{3,2,1,0:T(8,128)S(1)}, f32[3,16,32,128]{3,2,1,0:T(8,128)}, u32[]{:S(2)}) copy-start(f32[3,16,32,128]{3,2,1,0:T(8,128)} %param.4) | copy-start | bytes 2359300
  22.8 12.7 %collective-permute-start.4 = (f32[3,8,32,128]{3,2,1,0:T(8,128)S(1)}, f32[3,8,32,128]{3,2,1,0:T(8,128)S(1)}, u32[]{:S(2)}, u32[]{:S(2)}) collective-permute-start(f32[3,8,32,128]{3,2,1,0:T(8,128)S(1)} %pad_maximum_fusion.30), channel_id=1, source_target_pairs={{4,0},{8,4},{12,8},{16,12},{20,16},{24,20},{28,24},{5,1},{9,5},{13... | collective-permute-start | bytes 1179656 | tf_op jit(solution)/shard_map/ppermute | solution.py:20
  35.9 7.6 %collective-permute-start.6 = (f32[3,2,32,128]{3,2,1,0:T(8,128)S(1)}, f32[3,2,32,128]{3,2,1,0:T(8,128)S(1)}, u32[]{:S(2)}, u32[]{:S(2)}) collective-permute-start(f32[3,2,32,128]{3,2,1,0:T(8,128)S(1)} %get-tuple-element.66), channel_id=1, source_target_pairs={{4,0},{8,4},{12,8},{16,12},{20,16},{24,20},{28,24},{5,1},{9,5},{13... | collective-permute-start | bytes 294920 | tf_op jit(solution)/shard_map/ppermute | solution.py:31
  37.2 8.8 %collective-permute-start.5 = (f32[3,2,32,128]{3,2,1,0:T(8,128)S(1)}, f32[3,2,32,128]{3,2,1,0:T(8,128)S(1)}, u32[]{:S(2)}, u32[]{:S(2)}) collective-permute-start(f32[3,2,32,128]{3,2,1,0:T(8,128)S(1)} %get-tuple-element.65), channel_id=1, source_target_pairs={{0,4},{4,8},{8,12},{12,16},{16,20},{20,24},{24,28},{1,5},{5,9},{9,... | collective-permute-start | bytes 294920 | tf_op jit(solution)/shard_map/ppermute | solution.py:28
  46.0 5.6 %collective-permute-start.8 = (f32[3,20,2,128]{3,2,1,0:T(2,128)S(1)}, f32[3,20,2,128]{3,2,1,0:T(2,128)S(1)}, u32[]{:S(2)}, u32[]{:S(2)}) collective-permute-start(f32[3,20,2,128]{3,2,1,0:T(2,128)S(1)} %get-tuple-element.58), channel_id=1, source_target_pairs={{1,0},{2,1},{3,2},{5,4},{6,5},{7,6},{9,8},{10,9},{11,10},{13,12},{... | collective-permute-start | bytes 184328 | tf_op jit(solution)/shard_map/ppermute | solution.py:31
  48.4 4.5 %collective-permute-start.7 = (f32[3,20,2,128]{3,2,1,0:T(2,128)S(1)}, f32[3,20,2,128]{3,2,1,0:T(2,128)S(1)}, u32[]{:S(2)}, u32[]{:S(2)}) collective-permute-start(f32[3,20,2,128]{3,2,1,0:T(2,128)S(1)} %get-tuple-element.57), channel_id=1, source_target_pairs={{0,1},{1,2},{2,3},{4,5},{5,6},{6,7},{8,9},{9,10},{10,11},{12,13},{... | collective-permute-start | bytes 184328 | tf_op jit(solution)/shard_map/ppermute | solution.py:28
  57.0 12.5 %collective-permute-start.9 = (f32[3,8,32,128]{3,2,1,0:T(8,128)S(1)}, f32[3,8,32,128]{3,2,1,0:T(8,128)S(1)}, u32[]{:S(2)}, u32[]{:S(2)}) collective-permute-start(f32[3,8,32,128]{3,2,1,0:T(8,128)S(1)} %pad_maximum_fusion.28), channel_id=1, source_target_pairs={{4,0},{8,4},{12,8},{16,12},{20,16},{24,20},{28,24},{5,1},{9,5},{13... | collective-permute-start | bytes 1179656 | tf_op jit(solution)/shard_map/ppermute | solution.py:20
  69.8 7.7 %collective-permute-start.11 = (f32[3,2,32,128]{3,2,1,0:T(8,128)S(1)}, f32[3,2,32,128]{3,2,1,0:T(8,128)S(1)}, u32[]{:S(2)}, u32[]{:S(2)}) collective-permute-start(f32[3,2,32,128]{3,2,1,0:T(8,128)S(1)} %get-tuple-element.64), channel_id=1, source_target_pairs={{4,0},{8,4},{12,8},{16,12},{20,16},{24,20},{28,24},{5,1},{9,5},{13... | collective-permute-start | bytes 294920 | tf_op jit(solution)/shard_map/ppermute | solution.py:31
  71.1 8.8 %collective-permute-start.10 = (f32[3,2,32,128]{3,2,1,0:T(8,128)S(1)}, f32[3,2,32,128]{3,2,1,0:T(8,128)S(1)}, u32[]{:S(2)}, u32[]{:S(2)}) collective-permute-start(f32[3,2,32,128]{3,2,1,0:T(8,128)S(1)} %get-tuple-element.63), channel_id=1, source_target_pairs={{0,4},{4,8},{8,12},{12,16},{16,20},{20,24},{24,28},{1,5},{5,9},{9,... | collective-permute-start | bytes 294920 | tf_op jit(solution)/shard_map/ppermute | solution.py:28
  79.9 5.8 %collective-permute-start.13 = (f32[3,20,2,128]{3,2,1,0:T(2,128)S(1)}, f32[3,20,2,128]{3,2,1,0:T(2,128)S(1)}, u32[]{:S(2)}, u32[]{:S(2)}) collective-permute-start(f32[3,20,2,128]{3,2,1,0:T(2,128)S(1)} %get-tuple-element.56), channel_id=1, source_target_pairs={{1,0},{2,1},{3,2},{5,4},{6,5},{7,6},{9,8},{10,9},{11,10},{13,12},{... | collective-permute-start | bytes 184328 | tf_op jit(solution)/shard_map/ppermute | solution.py:31
  82.3 4.5 %collective-permute-start.12 = (f32[3,20,2,128]{3,2,1,0:T(2,128)S(1)}, f32[3,20,2,128]{3,2,1,0:T(2,128)S(1)}, u32[]{:S(2)}, u32[]{:S(2)}) collective-permute-start(f32[3,20,2,128]{3,2,1,0:T(2,128)S(1)} %get-tuple-element.55), channel_id=1, source_target_pairs={{0,1},{1,2},{2,3},{4,5},{5,6},{6,7},{8,9},{9,10},{10,11},{12,13},{... | collective-permute-start | bytes 184328 | tf_op jit(solution)/shard_map/ppermute | solution.py:28
  90.9 12.5 %collective-permute-start.14 = (f32[3,8,32,128]{3,2,1,0:T(8,128)S(1)}, f32[3,8,32,128]{3,2,1,0:T(8,128)S(1)}, u32[]{:S(2)}, u32[]{:S(2)}) collective-permute-start(f32[3,8,32,128]{3,2,1,0:T(8,128)S(1)} %pad_maximum_fusion.26), channel_id=1, source_target_pairs={{4,0},{8,4},{12,8},{16,12},{20,16},{24,20},{28,24},{5,1},{9,5},{13... | collective-permute-start | bytes 1179656 | tf_op jit(solution)/shard_map/ppermute | solution.py:20
  103.7 7.7 %collective-permute-start.16 = (f32[3,2,32,128]{3,2,1,0:T(8,128)S(1)}, f32[3,2,32,128]{3,2,1,0:T(8,128)S(1)}, u32[]{:S(2)}, u32[]{:S(2)}) collective-permute-start(f32[3,2,32,128]{3,2,1,0:T(8,128)S(1)} %get-tuple-element.62), channel_id=1, source_target_pairs={{4,0},{8,4},{12,8},{16,12},{20,16},{24,20},{28,24},{5,1},{9,5},{13... | collective-permute-start | bytes 294920 | tf_op jit(solution)/shard_map/ppermute | solution.py:31
  105.0 8.8 %collective-permute-start.15 = (f32[3,2,32,128]{3,2,1,0:T(8,128)S(1)}, f32[3,2,32,128]{3,2,1,0:T(8,128)S(1)}, u32[]{:S(2)}, u32[]{:S(2)}) collective-permute-start(f32[3,2,32,128]{3,2,1,0:T(8,128)S(1)} %get-tuple-element.61), channel_id=1, source_target_pairs={{0,4},{4,8},{8,12},{12,16},{16,20},{20,24},{24,28},{1,5},{5,9},{9,... | collective-permute-start | bytes 294920 | tf_op jit(solution)/shard_map/ppermute | solution.py:28
  113.8 5.6 %collective-permute-start.18 = (f32[3,20,2,128]{3,2,1,0:T(2,128)S(1)}, f32[3,20,2,128]{3,2,1,0:T(2,128)S(1)}, u32[]{:S(2)}, u32[]{:S(2)}) collective-permute-start(f32[3,20,2,128]{3,2,1,0:T(2,128)S(1)} %get-tuple-element.54), channel_id=1, source_target_pairs={{1,0},{2,1},{3,2},{5,4},{6,5},{7,6},{9,8},{10,9},{11,10},{13,12},{... | collective-permute-start | bytes 184328 | tf_op jit(solution)/shard_map/ppermute | solution.py:31
  116.2 4.5 %collective-permute-start.17 = (f32[3,20,2,128]{3,2,1,0:T(2,128)S(1)}, f32[3,20,2,128]{3,2,1,0:T(2,128)S(1)}, u32[]{:S(2)}, u32[]{:S(2)}) collective-permute-start(f32[3,20,2,128]{3,2,1,0:T(2,128)S(1)} %get-tuple-element.53), channel_id=1, source_target_pairs={{0,1},{1,2},{2,3},{4,5},{5,6},{6,7},{8,9},{9,10},{10,11},{12,13},{... | collective-permute-start | bytes 184328 | tf_op jit(solution)/shard_map/ppermute | solution.py:28
  124.8 12.5 %collective-permute-start.19 = (f32[3,8,32,128]{3,2,1,0:T(8,128)S(1)}, f32[3,8,32,128]{3,2,1,0:T(8,128)S(1)}, u32[]{:S(2)}, u32[]{:S(2)}) collective-permute-start(f32[3,8,32,128]{3,2,1,0:T(8,128)S(1)} %pad_maximum_fusion.24), channel_id=1, source_target_pairs={{4,0},{8,4},{12,8},{16,12},{20,16},{24,20},{28,24},{5,1},{9,5},{13... | collective-permute-start | bytes 1179656 | tf_op jit(solution)/shard_map/ppermute | solution.py:20
where the time goes:
time: 140 us; the launch traced here: 138 us
  starting transfers between devices  53.9 us (38%)
  waiting for transfers between devices  45.9 us (33%)
  between operations  15.5 us (11%)
  other arithmetic  14.8 us (11%)
  local copies, waits for them, and re-layouts  8.36 us (6%)
    ppermute x8, starting transfers between devices, with_halo(): lax.ppermute(lax.slice_in_dim(block, block.shape[dim] - width, None, axis...  32.2 us
    ppermute x4, waiting for transfers between devices, passed_along(): lax.ppermute(value, axis, [(source, source + steps) for source in range(l...  27.4 us
    ppermute x8, starting transfers between devices, with_halo(): lax.ppermute(lax.slice_in_dim(block, 0, width, axis=dim), axis, backward)  16.3 us
    ppermute x8, waiting for transfers between devices, with_halo(): lax.ppermute(lax.slice_in_dim(block, block.shape[dim] - width, None, axis...  12.4 us
    ppermute x8, waiting for transfers between devices, with_halo(): lax.ppermute(lax.slice_in_dim(block, 0, width, axis=dim), axis, backward)  6.13 us
    sub x8, other arithmetic, advance(): padded[:, 2:, 1:-1] + padded[:, :-2, 1:-1] + padded[:, 1:-1, 2:]  6.09 us
    slice x16, local copies, waits for them, and re-layouts, advance(): jnp.roll(centre, -1, 3)  5.45 us
    ppermute x4, starting transfers between devices, passed_along(): lax.ppermute(value, axis, [(source, source + steps) for source in range(l...  5.3 us
  transfers between devices with their start and end apart: 20, of which 16 were waited for; matrix products, arithmetic and copies ran while one was open for 3% of the time, Pallas kernels for 0%

commit v1 on v0

v1 whole, which is shorter than its diff:
```python
import jax
import jax.numpy as jnp
from jax import lax
from jax.experimental import pallas as pl
from jax.experimental.pallas import tpu as pltpu
from jax.sharding import PartitionSpec as P

TILE = 8
GROUP = 6

coef_phase = 0.15
coef_react = 0.3
coef_couple = 0.4
coef_solute = 1.5
coef_diff = 0.1
coef_heat = 0.16


def passed(value, grow_step, wide_pairs=None):
    grow, wide = lax.axis_size("grow"), lax.axis_size("wide")
    if wide_pairs is None:
        return lax.ppermute(value, "grow", [(g, g + grow_step) for g in range(grow) if 0 <= g + grow_step < grow])
    lanes = wide_pairs + [(b, a) for a, b in wide_pairs]
    if grow_step == 0:
        return lax.ppermute(value, "wide", lanes)
    pairs = [
        (g * wide + a, (g + grow_step) * wide + b)
        for g in range(grow)
        if 0 <= g + grow_step < grow
        for a, b in lanes
    ]
    return lax.ppermute(value, ("grow", "wide"), pairs)


def evolve_kernel(slide_ref, own, near, far, melt, outer_own, outer_melt, outer_near, outer_far,
                  inner_own, inner_melt, inner_near, inner_far, out, even, odd, sems, out_sem):
    rows, cols = own.shape[1], own.shape[2]
    steps = slide_ref.shape[0]
    reach = steps
    count = rows + 2 * reach
    zero_slot = count + 2 * reach
    first_col = 2 * TILE
    total_rows = rows * lax.axis_size("grow")
    grow_index, wide_index = lax.axis_index("grow"), lax.axis_index("wide")
    at_end = grow_index == lax.axis_size("grow") - 1
    next_end = grow_index == lax.axis_size("grow") - 2
    is_even = lax.rem(wide_index, 2) == 0
    low_inside = wide_index > 0
    high_inside = wide_index < lax.axis_size("wide") - 1

    total = slide_ref[0]
    for k in range(1, steps):
        total = total + slide_ref[k]
    extra = total - reach
    base = grow_index * rows + extra - reach
    low_col, high_col = first_col - reach, first_col + cols
    outer_col = pl.multiple_of(jnp.where(is_even, low_col, high_col), TILE)
    inner_col = pl.multiple_of(jnp.where(is_even, high_col, low_col), TILE)

    def fetch(source, first, length, col, width, sem):
        return pltpu.make_async_copy(
            source.at[:, pl.ds(0, length)],
            even.at[:, pl.ds(reach - extra + first, length), pl.ds(col, width)],
            sems.at[sem],
        )

    def part(first, length, block, outer, inner, sem):
        return [
            fetch(block, first, length, first_col, cols, sem),
            fetch(outer, first, length, outer_col, reach, sem + 1),
            fetch(inner, first, length, inner_col, reach, sem + 2),
        ]

    near_len, far_len = near.shape[1], far.shape[1]
    own_part = part(0, rows, own, outer_own, inner_own, 0)
    near_part = part(rows, near_len, near, outer_near, inner_near, 3)
    near_melt = part(rows, near_len, melt, outer_melt, inner_melt, 3)
    far_part = part(2 * rows, far_len, far, outer_far, inner_far, 6)
    far_melt = part(2 * rows, far_len, melt, outer_melt, inner_melt, 6)

    def both(act):
        for copy in own_part:
            act(copy)

        @pl.when(at_end)
        def _():
            for copy in near_melt:
                act(copy)

        @pl.when(jnp.logical_not(at_end))
        def _():
            for copy in near_part:
                act(copy)

        @pl.when(next_end)
        def _():
            for copy in far_melt:
                act(copy)

        @pl.when(jnp.logical_not(next_end))
        def _():
            for copy in far_part:
                act(copy)

    both(lambda copy: copy.start())
    for field in range(3):
        for buffer in (even, odd):
            buffer[field, zero_slot] = jnp.zeros_like(buffer[field, zero_slot])
    both(lambda copy: copy.wait())

    tiles = cols // TILE + 2 * (reach // TILE)
    first_row = first_col - reach
    cursor = jnp.int32(0)
    for k in range(steps):
        source, target = (even, odd) if k % 2 == 0 else (odd, even)
        next_cursor = cursor + slide_ref[k]
        top = cursor + total_rows - base
        bottom = next_cursor - base
        last = k == steps - 1
        low, high = reach + k + 1, reach + count - 1 - k
        live_low = jnp.clip(bottom, low, high)
        live_high = jnp.clip(top, live_low, high)

        def group(j, carry):
            r = live_low + GROUP * j
            slots = [r - 1, r] + [jnp.where(r + q < top, r + q, zero_slot) for q in range(1, GROUP + 1)]
            for t in range(1, tiles - 1) if last else range(tiles):
                s0 = first_row + TILE * t
                centre = [[source[f, slot, pl.ds(s0, TILE)] for slot in slots] for f in range(3)]
                for i in range(GROUP):
                    slot = slots[1 + i]
                    value, around = [], []
                    for f in range(3):
                        c = centre[f][1 + i]
                        around.append(
                            (centre[f][i] + centre[f][i + 2])
                            + (source[f, slot, pl.ds(s0 - 1, TILE)] + source[f, slot, pl.ds(s0 + 1, TILE)])
                            + (pltpu.roll(c, 1, 1) + pltpu.roll(c, c.shape[1] - 1, 1))
                        )
                        value.append(c)
                    phase, solute, heat = value
                    squared = phase * phase
                    rest = 1.0 - squared
                    drive = (
                        coef_phase * around[0]
                        + phase * ((1.0 - 6.0 * coef_phase + coef_react) - coef_react * squared)
                        - (rest * rest) * (coef_couple * heat + (coef_couple * coef_solute) * solute)
                    )
                    grown = jnp.tanh(drive)
                    change = 0.5 * (grown - phase)
                    result = [
                        grown,
                        (1.0 - 6.0 * coef_diff) * solute + (coef_diff * around[1] + change),
                        (1.0 - 6.0 * coef_heat) * heat + (coef_heat * around[2] + change),
                    ]
                    if t == 0:
                        result = [jnp.where(low_inside, v, 0.0) for v in result]
                    if t == tiles - 1:
                        result = [jnp.where(high_inside, v, 0.0) for v in result]
                    for f in range(3):
                        target[f, r + i, pl.ds(s0, TILE)] = result[f]
            return carry

        lax.fori_loop(0, (live_high - live_low + GROUP - 1) // GROUP, group, 0)

        def clear(r, carry):
            for f in range(3):
                target[f, r, pl.ds(first_row, TILE * tiles)] = jnp.zeros((TILE * tiles, target.shape[3]), jnp.float32)
            return carry

        def keep(r, carry):
            for f in range(3):
                target[f, r, pl.ds(first_row, TILE * tiles)] = source[f, r, pl.ds(first_row, TILE * tiles)]
            return carry

        lax.fori_loop(low, live_low, clear, 0)
        lax.fori_loop(live_high, high, keep, 0)
        cursor = next_cursor

    final = even if steps % 2 == 0 else odd
    copy = pltpu.make_async_copy(final.at[:, pl.ds(2 * reach, rows), pl.ds(first_col, cols)], out, out_sem)
    copy.start()
    copy.wait()


def evolve(slide_planes, *arrays):
    own = arrays[0]
    rows, cols, depth = own.shape[1:]
    reach = slide_planes.shape[0]
    buffer = pltpu.VMEM((3, rows + 4 * reach + 1, cols + 4 * TILE, depth), jnp.float32)
    anywhere = pl.BlockSpec(memory_space=pl.ANY)
    return pl.pallas_call(
        evolve_kernel,
        out_shape=jax.ShapeDtypeStruct(own.shape, own.dtype),
        in_specs=[pl.BlockSpec(memory_space=pltpu.SMEM)] + [anywhere] * len(arrays),
        out_specs=anywhere,
        scratch_shapes=[buffer, buffer, pltpu.SemaphoreType.DMA((9,)), pltpu.SemaphoreType.DMA],
        compiler_params=pltpu.CompilerParams(vmem_limit_bytes=40 * 1024 * 1024),
    )(slide_planes, *arrays)


def body(fields, melt_planes, slide_planes):
    rows, cols = fields.shape[1], fields.shape[2]
    reach = slide_planes.shape[0]
    wide = lax.axis_size("wide")
    inner_pairs = [(a, a + 1) for a in range(0, wide - 1, 2)]
    outer_pairs = [(a, a + 1) for a in range(1, wide - 1, 2)]
    is_even = lax.rem(lax.axis_index("wide"), 2) == 0
    outer_start = jnp.where(is_even, 0, cols - reach)
    inner_start = jnp.where(is_even, cols - reach, 0)

    def edge(block, start):
        return lax.dynamic_slice_in_dim(block, start, reach, 2)

    near = passed(fields, -1)
    outer = edge(fields, outer_start)
    outer_near = passed(outer, -1, outer_pairs)
    far = passed(fields[:, :reach], -2)
    outer_far = passed(outer[:, :reach], -2, outer_pairs)
    outer_own = passed(outer, 0, outer_pairs)
    outer_melt = passed(edge(melt_planes, outer_start), 0, outer_pairs)
    inner_own = passed(edge(fields, inner_start), 0, inner_pairs)
    inner_melt = passed(edge(melt_planes, inner_start), 0, inner_pairs)
    inner_near = passed(edge(near, inner_start), 0, inner_pairs)
    inner_far = passed(edge(far, inner_start), 0, inner_pairs)
    return evolve(
        slide_planes, fields, near, far, melt_planes,
        outer_own, outer_melt, outer_near, outer_far,
        inner_own, inner_melt, inner_near, inner_far,
    )


def solution(mesh):
    return jax.shard_map(
        body,
        mesh=mesh,
        in_specs=(P(None, "grow", "wide", None), P(None, None, "wide", None), P()),
        out_specs=P(None, "grow", "wide", None),
        check_vma=False,
    )
```

time: 140 us -> 52.2 us (0.37); the launches traced: 138 us -> 52.2 us
  starting transfers between devices: 53.9 us -> 13.3 us
  waiting for transfers between devices: 45.9 us -> 25 us
  between operations: 15.5 us -> 0.18 us
  other arithmetic: 14.8 us -> 0 us
  Pallas kernels: 0 us -> 11.5 us
  local copies, waits for them, and re-layouts: 8.36 us -> 2.23 us
    ppermute x20 -> x10, starting transfers between devices: 53.9 us -> 13.3 us  [the longest x6 8.05 us: passed(): return lax.ppermute(value, 'wide', lanes)]
    ppermute x20 -> x10, waiting for transfers between devices: 45.9 us -> 25 us  [the longest x2 10.8 us: passed(): return lax.ppermute(value, ('grow', 'wide'), pairs)]
    pallas_call x0 -> x1, Pallas kernels: none -> 11.5 us  [evolve(): pl.pallas_call(evolve_kernel, out_shape=jax.ShapeDtypeStruct(own.shape, o...]
    slice x22 -> x2, local copies, waits for them, and re-layouts: 7.15 us -> 1.05 us  [the longest x1 1.03 us: body(): far = passed(fields[:, :reach], -2)]
    sub x8 -> x0, other arithmetic: 6.09 us -> none  [advance(): padded[:, 2:, 1:-1] + padded[:, :-2, 1:-1] + padded[:, 1:-1, 2:]]
    add x16 -> x0, other arithmetic: 3.1 us -> none  [the longest x8 1.67 us: advance(): solute_next = solute + coef_diff * laplace[1] + change]
    concatenate x8 -> x0, other arithmetic: 2.44 us -> none  [the longest x4 1.67 us: slide_block(): combined = jnp.concatenate([state, incoming], 1)]
    reduce_sum x3 -> x0, other arithmetic: 1.89 us -> none  [body(): cursor = jnp.sum(slide_planes[:substep])]
  transfers between devices with their start and end apart: 20 -> 10, of which waited for: 16 -> 4; matrix products, arithmetic and copies ran while one was open for 3% -> 4% of each run, Pallas kernels for 0% -> 0%
where the time goes in v1:
time: 52.2 us
  waiting for transfers between devices  25 us (48%)
  starting transfers between devices  13.3 us (25%)
  Pallas kernels  11.5 us (22%)
  local copies, waits for them, and re-layouts  2.23 us (4%)
    pallas_call x1, Pallas kernels, evolve(): pl.pallas_call(evolve_kernel, out_shape=jax.ShapeDtypeStruct(own.shape, o...  11.5 us
    ppermute x2, waiting for transfers between devices, passed(): return lax.ppermute(value, ('grow', 'wide'), pairs)  10.8 us
    ppermute x2, waiting for transfers between devices, passed(): lax.ppermute(value, 'grow', [(g, g + grow_step) for g in range(grow) if 0...  10.5 us
    ppermute x6, starting transfers between devices, passed(): return lax.ppermute(value, 'wide', lanes)  8.05 us
    ppermute x6, waiting for transfers between devices, passed(): return lax.ppermute(value, 'wide', lanes)  3.6 us
    ppermute x2, starting transfers between devices, passed(): lax.ppermute(value, 'grow', [(g, g + grow_step) for g in range(grow) if 0...  2.7 us
    ppermute x2, starting transfers between devices, passed(): return lax.ppermute(value, ('grow', 'wide'), pairs)  2.57 us
    dynamic_slice x4, local copies, waits for them, and re-layouts, edge(): return lax.dynamic_slice_in_dim(block, start, reach, 2)  1.17 us
  transfers between devices with their start and end apart: 10, of which 4 were waited for; matrix products, arithmetic and copies ran while one was open for 4% of the time, Pallas kernels for 0%

profile of v1, /device:TPU:1, one launch (start us, length us, event | category | flops | bytes accessed | tf_op | source)
XLA Modules:
  0.0 52.2 jit_solution(11621440523450499282)
XLA Ops:
  0.0 0.0 copy-start
  0.0 1.4 %collective-permute-start = (f32[3,16,32,128]{3,2,1,0:T(8,128)}, f32[3,16,32,128]{3,2,1,0:T(8,128)S(1)}, u32[]{:S(2)}, u32[]{:S(2)}) collective-permute-start(f32[3,16,32,128]{3,2,1,0:T(8,128)} %own.1), channel_id=1, source_target_pairs={{4,0},{8,4},{12,8},{16,12},{20,16},{24,20},{28,24},{5,1},{9,5},{13... | collective-permute-start | bytes 2359304 | tf_op jit(solution)/shard_map/ppermute | solution.py:22
  1.4 1.0 %slice.6 = f32[3,8,32,128]{3,2,1,0:T(8,128)S(1)} slice(f32[3,16,32,128]{3,2,1,0:T(8,128)} %own.1), slice={[0:3], [0:8], [0:32], [0:128]} | slice | bytes 786432 | tf_op jit(solution)/shard_map/slice | solution.py:218
  2.5 1.3 %collective-permute-start.1 = (f32[3,8,32,128]{3,2,1,0:T(8,128)S(1)}, f32[3,8,32,128]{3,2,1,0:T(8,128)S(1)}, u32[]{:S(2)}, u32[]{:S(2)}) collective-permute-start(f32[3,8,32,128]{3,2,1,0:T(8,128)S(1)} %slice.6), channel_id=1, source_target_pairs={{8,0},{12,4},{16,8},{20,12},{24,16},{28,20},{9,1},{13,5},{17,9},{2... | collective-permute-start | bytes 1179656 | tf_op jit(solution)/shard_map/ppermute | solution.py:22
  3.8 0.0 copy-done
  3.8 1.3 %collective-permute-start.5 = (f32[3,8,8,128]{3,2,1,0:T(8,128)S(1)}, f32[3,8,8,128]{3,2,1,0:T(8,128)S(1)}, u32[]{:S(2)}, u32[]{:S(2)}) collective-permute-start(f32[3,8,8,128]{3,2,1,0:T(8,128)S(1)} %constant_dynamic-slice_fusion), channel_id=1, source_target_pairs={{9,2},{10,1},{13,6},{14,5},{17,10},{18,9},{21,14},{22,13},{25,18},... | collective-permute-start | bytes 294920 | tf_op jit(solution)/shard_map/ppermute | solution.py:32
  5.1 1.1 %constant_dynamic-slice_fusion.3 = (f32[3,16,8,128]{3,2,1,0:T(8,128)S(1)}, f32[3,16,8,128]{3,2,1,0:T(8,128)S(1)}) fusion(f32[3,16,32,128]{3,2,1,0:T(8,128)} %melt.1, s32[]{:T(128)S(6)} %select_n.14, s32[]{:T(128)S(6)} %select_n.7), kind=kLoop, calls=%fused_computation.3 | loop fusion | bytes 786440 | tf_op jit(solution)/shard_map/dynamic_slice | solution.py:213
  6.2 0.0 copy-start.1
  6.2 0.1 collective-permute-start.7
  6.3 4.7 %collective-permute-start.3 = (f32[3,16,8,128]{3,2,1,0:T(8,128)S(1)}, f32[3,16,8,128]{3,2,1,0:T(8,128)S(1)}, u32[]{:S(2)}, u32[]{:S(2)}) collective-permute-start(f32[3,16,8,128]{3,2,1,0:T(8,128)S(1)} %get-tuple-element.6), channel_id=1, source_target_pairs={{1,2},{2,1},{5,6},{6,5},{9,10},{10,9},{13,14},{14,13},{17,18},{18,... | collective-permute-start | bytes 589832 | tf_op jit(solution)/shard_map/ppermute | solution.py:25
  10.9 0.1 constant_dynamic-slice_fusion.4
  11.0 10.5 %collective-permute-done.near = f32[3,16,32,128]{3,2,1,0:T(8,128)S(1)} collective-permute-done((f32[3,16,32,128]{3,2,1,0:T(8,128)}, f32[3,16,32,128]{3,2,1,0:T(8,128)S(1)}, u32[]{:S(2)}, u32[]{:S(2)}) %collective-permute-start) | collective-permute-done | bytes 786464 | tf_op jit(solution)/shard_map/ppermute | solution.py:22
  21.5 1.3 %collective-permute-start.4 = (f32[3,16,8,128]{3,2,1,0:T(8,128)S(1)}, f32[3,16,8,128]{3,2,1,0:T(8,128)S(1)}, u32[]{:S(2)}, u32[]{:S(2)}) collective-permute-start(f32[3,16,8,128]{3,2,1,0:T(8,128)S(1)} %get-tuple-element.8), channel_id=1, source_target_pairs={{5,2},{6,1},{9,6},{10,5},{13,10},{14,9},{17,14},{18,13},{21,18},{2... | collective-permute-start | bytes 589832 | tf_op jit(solution)/shard_map/ppermute | solution.py:32
  22.9 10.8 %collective-permute-done.5.outer_far = f32[3,8,8,128]{3,2,1,0:T(8,128)S(1)} collective-permute-done((f32[3,8,8,128]{3,2,1,0:T(8,128)S(1)}, f32[3,8,8,128]{3,2,1,0:T(8,128)S(1)}, u32[]{:S(2)}, u32[]{:S(2)}) %collective-permute-start.5) | collective-permute-done | bytes 98336 | tf_op jit(solution)/shard_map/ppermute | solution.py:32
  33.7 2.6 %collective-permute-start.2 = (f32[3,16,8,128]{3,2,1,0:T(8,128)S(1)}, f32[3,16,8,128]{3,2,1,0:T(8,128)S(1)}, u32[]{:S(2)}, u32[]{:S(2)}) collective-permute-start(f32[3,16,8,128]{3,2,1,0:T(8,128)S(1)} %get-tuple-element.8), channel_id=1, source_target_pairs={{1,2},{2,1},{5,6},{6,5},{9,10},{10,9},{13,14},{14,13},{17,18},{18,... | collective-permute-start | bytes 589832 | tf_op jit(solution)/shard_map/ppermute | solution.py:25
  36.3 0.0 collective-permute-done.7.inner_melt
  36.3 0.0 copy-start.2
  36.3 0.1 collective-permute-start.6
  36.4 0.0 collective-permute-done.1.far
  36.4 0.5 collective-permute-start.8
  36.9 0.0 collective-permute-done.3.outer_melt
  36.9 0.2 collective-permute-start.9
  37.1 0.7 %collective-permute-done.6.inner_own = f32[3,16,8,128]{3,2,1,0:T(8,128)S(1)} collective-permute-done((f32[3,16,8,128]{3,2,1,0:T(8,128)S(1)}, f32[3,16,8,128]{3,2,1,0:T(8,128)S(1)}, u32[]{:S(2)}, u32[]{:S(2)}) %collective-permute-start.6) | collective-permute-done | bytes 196640 | tf_op jit(solution)/shard_map/ppermute | solution.py:25
  37.8 0.0 collective-permute-done.4.outer_near
  37.8 2.8 %collective-permute-done.2.outer_own = f32[3,16,8,128]{3,2,1,0:T(8,128)S(1)} collective-permute-done((f32[3,16,8,128]{3,2,1,0:T(8,128)S(1)}, f32[3,16,8,128]{3,2,1,0:T(8,128)S(1)}, u32[]{:S(2)}, u32[]{:S(2)}) %collective-permute-start.2) | collective-permute-done | bytes 196640 | tf_op jit(solution)/shard_map/ppermute | solution.py:25
  40.7 0.0 collective-permute-done.9.inner_far
  40.7 0.0 collective-permute-done.8.inner_near
  40.7 0.0 copy-done.1
  40.7 0.0 copy-done.2
  40.7 11.5 %shard_map.37 = f32[3,16,32,128]{3,2,1,0:T(8,128)} custom-call(s32[8]{0:T(128)S(1)} %copy-done.2, f32[3,16,32,128]{3,2,1,0:T(8,128)S(1)} %copy-done, f32[3,16,32,128]{3,2,1,0:T(8,128)S(1)} %collective-permute-done.near, f32[3,8,32,128]{3,2,1,0:T(8,128)S(1)} %collective-permute-done.1.far, f32[3,16,32,128]{3,2,1,0:T(8,128)S(1)} %copy-done.1, ...), custom_call_target="tpu_custom_call" | custom-call | tf_op jit(solution)/shard_map/pallas_call | solution.py:192
  (3 shorter events, 0.1 us)
Async XLA Ops:
  0.0 3.8 %copy-start = (f32[3,16,32,128]{3,2,1,0:T(8,128)S(1)}, f32[3,16,32,128]{3,2,1,0:T(8,128)}, u32[]{:S(2)}) copy-start(f32[3,16,32,128]{3,2,1,0:T(8,128)} %own.1) | copy-start | bytes 2359300
  0.0 21.5 %collective-permute-start = (f32[3,16,32,128]{3,2,1,0:T(8,128)}, f32[3,16,32,128]{3,2,1,0:T(8,128)S(1)}, u32[]{:S(2)}, u32[]{:S(2)}) collective-permute-start(f32[3,16,32,128]{3,2,1,0:T(8,128)} %own.1), channel_id=1, source_target_pairs={{4,0},{8,4},{12,8},{16,12},{20,16},{24,20},{28,24},{5,1},{9,5},{13... | collective-permute-start | bytes 2359304 | tf_op jit(solution)/shard_map/ppermute | solution.py:22
  2.5 33.9 %collective-permute-start.1 = (f32[3,8,32,128]{3,2,1,0:T(8,128)S(1)}, f32[3,8,32,128]{3,2,1,0:T(8,128)S(1)}, u32[]{:S(2)}, u32[]{:S(2)}) collective-permute-start(f32[3,8,32,128]{3,2,1,0:T(8,128)S(1)} %slice.6), channel_id=1, source_target_pairs={{8,0},{12,4},{16,8},{20,12},{24,16},{28,20},{9,1},{13,5},{17,9},{2... | collective-permute-start | bytes 1179656 | tf_op jit(solution)/shard_map/ppermute | solution.py:22
  3.8 29.9 %collective-permute-start.5 = (f32[3,8,8,128]{3,2,1,0:T(8,128)S(1)}, f32[3,8,8,128]{3,2,1,0:T(8,128)S(1)}, u32[]{:S(2)}, u32[]{:S(2)}) collective-permute-start(f32[3,8,8,128]{3,2,1,0:T(8,128)S(1)} %constant_dynamic-slice_fusion), channel_id=1, source_target_pairs={{9,2},{10,1},{13,6},{14,5},{17,10},{18,9},{21,14},{22,13},{25,18},... | collective-permute-start | bytes 294920 | tf_op jit(solution)/shard_map/ppermute | solution.py:32
  6.2 34.5 %copy-start.1 = (f32[3,16,32,128]{3,2,1,0:T(8,128)S(1)}, f32[3,16,32,128]{3,2,1,0:T(8,128)}, u32[]{:S(2)}) copy-start(f32[3,16,32,128]{3,2,1,0:T(8,128)} %melt.1) | copy-start | bytes 2359300
  6.2 30.1 %collective-permute-start.7 = (f32[3,16,8,128]{3,2,1,0:T(8,128)S(1)}, f32[3,16,8,128]{3,2,1,0:T(8,128)S(1)}, u32[]{:S(2)}, u32[]{:S(2)}) collective-permute-start(f32[3,16,8,128]{3,2,1,0:T(8,128)S(1)} %get-tuple-element.5), channel_id=1, source_target_pairs={{0,1},{2,3},{1,0},{3,2},{4,5},{6,7},{5,4},{7,6},{8,9},{10,11},{9,8... | collective-permute-start | bytes 589832 | tf_op jit(solution)/shard_map/ppermute | solution.py:25
  6.3 30.7 %collective-permute-start.3 = (f32[3,16,8,128]{3,2,1,0:T(8,128)S(1)}, f32[3,16,8,128]{3,2,1,0:T(8,128)S(1)}, u32[]{:S(2)}, u32[]{:S(2)}) collective-permute-start(f32[3,16,8,128]{3,2,1,0:T(8,128)S(1)} %get-tuple-element.6), channel_id=1, source_target_pairs={{1,2},{2,1},{5,6},{6,5},{9,10},{10,9},{13,14},{14,13},{17,18},{18,... | collective-permute-start | bytes 589832 | tf_op jit(solution)/shard_map/ppermute | solution.py:25
  21.5 16.3 %collective-permute-start.4 = (f32[3,16,8,128]{3,2,1,0:T(8,128)S(1)}, f32[3,16,8,128]{3,2,1,0:T(8,128)S(1)}, u32[]{:S(2)}, u32[]{:S(2)}) collective-permute-start(f32[3,16,8,128]{3,2,1,0:T(8,128)S(1)} %get-tuple-element.8), channel_id=1, source_target_pairs={{5,2},{6,1},{9,6},{10,5},{13,10},{14,9},{17,14},{18,13},{21,18},{2... | collective-permute-start | bytes 589832 | tf_op jit(solution)/shard_map/ppermute | solution.py:32
  33.7 7.0 %collective-permute-start.2 = (f32[3,16,8,128]{3,2,1,0:T(8,128)S(1)}, f32[3,16,8,128]{3,2,1,0:T(8,128)S(1)}, u32[]{:S(2)}, u32[]{:S(2)}) collective-permute-start(f32[3,16,8,128]{3,2,1,0:T(8,128)S(1)} %get-tuple-element.8), channel_id=1, source_target_pairs={{1,2},{2,1},{5,6},{6,5},{9,10},{10,9},{13,14},{14,13},{17,18},{18,... | collective-permute-start | bytes 589832 | tf_op jit(solution)/shard_map/ppermute | solution.py:25
  36.3 4.4 %copy-start.2 = (s32[8]{0:T(128)S(1)}, s32[8]{0:T(128)}, u32[]{:S(2)}) copy-start(s32[8]{0:T(128)} %slide_ref.1) | copy-start | bytes 100
  36.3 1.5 %collective-permute-start.6 = (f32[3,16,8,128]{3,2,1,0:T(8,128)S(1)}, f32[3,16,8,128]{3,2,1,0:T(8,128)S(1)}, u32[]{:S(2)}, u32[]{:S(2)}) collective-permute-start(f32[3,16,8,128]{3,2,1,0:T(8,128)S(1)} %get-tuple-element.7), channel_id=1, source_target_pairs={{0,1},{2,3},{1,0},{3,2},{4,5},{6,7},{5,4},{7,6},{8,9},{10,11},{9,8... | collective-permute-start | bytes 589832 | tf_op jit(solution)/shard_map/ppermute | solution.py:25
  36.4 4.3 %collective-permute-start.8 = (f32[3,16,8,128]{3,2,1,0:T(8,128)S(1)}, f32[3,16,8,128]{3,2,1,0:T(8,128)S(1)}, u32[]{:S(2)}, u32[]{:S(2)}) collective-permute-start(f32[3,16,8,128]{3,2,1,0:T(8,128)S(1)} %constant_dynamic-slice_fusion.2), channel_id=1, source_target_pairs={{0,1},{2,3},{1,0},{3,2},{4,5},{6,7},{5,4},{7,6},{8,9},{10,11},{9,8... | collective-permute-start | bytes 589832 | tf_op jit(solution)/shard_map/ppermute | solution.py:25
  36.9 3.7 %collective-permute-start.9 = (f32[3,8,8,128]{3,2,1,0:T(8,128)S(1)}, f32[3,8,8,128]{3,2,1,0:T(8,128)S(1)}, u32[]{:S(2)}, u32[]{:S(2)}) collective-permute-start(f32[3,8,8,128]{3,2,1,0:T(8,128)S(1)} %constant_dynamic-slice_fusion.1), channel_id=1, source_target_pairs={{0,1},{2,3},{1,0},{3,2},{4,5},{6,7},{5,4},{7,6},{8,9},{10,11},{9,8... | collective-permute-start | bytes 294920 | tf_op jit(solution)/shard_map/ppermute | solution.py:25
